TPU v7x, 32 devices: a whole 2x2x4 slice. The times are simulated.
32 devices in a mesh: segment: 4 (over y, x), node: 8 (over z, core).
Axes of the slice: x: 2, y: 2, z: 4, core: 2. Of those that a mesh axis runs over, the one named last changes fastest.
Arguments:
- activations: bfloat16 [4, 2048, 512], P('segment', 'node'), may hold values from -8 to 8
- norm_gain: float32 [4, 512], P('segment'), may hold values from 0.5 to 1.5
- project_in: bfloat16 [4, 512, 1536], P('segment'), may hold values from -0.25 to 0.25
- project_out: bfloat16 [4, 512, 512], P('segment'), may hold values from -0.5 to 0.5
- virtual_keys: bfloat16 [4, 4, 512], P('segment'), may hold values from -6 to 6
- virtual_id: int32 [2048, 1], P('node'), may hold values from 0 to 3
- local_rows: int32 [16, 2048], P(None, 'node'), may hold values from 0 to 127
- slot_block: int32 [16, 8], P('node'), may hold values from 0 to 15, as said below
- slot_count: int32 [16], P('node'), may hold values from 1 to 8, as said below
- slot_rows: int32 [16, 8, 4, 128], P('node'), may hold values from 0 to 127
Outputs:
- handed: bfloat16 [4, 2048, 512], P('segment', 'node')
Inputs may be any that keep to these rules, and one draw needn't show every extreme that they name: `virtual_id`: every virtual node has a member. `slot_block`: blocks d * 2 to (d + 1) * 2 - 1 lie on device d of node; every entry names a block of another device than the destination block's, and all entries of one device's rows that name blocks of the same device name the same block. `slot_count`: some block has 8 live slots.
All inputs are finite; a program needn't handle non-finite values.
Results may differ from a plain program's by a relative error of at most 0.0065.
Values may be sent and summed in bfloat16 or wider, within the bound.
No kernel may reach another device: no remote copies, remote signals or barrier semaphores. Data moves between devices by JAX's collectives and lax.ppermute only.
A program may use at most 64 MiB of HBM per device.

v0:
```python
import jax
import jax.numpy as jnp
from jax import lax
from jax.sharding import PartitionSpec as P

HEADS = 8


cap_limit = 10.0
epsilon = 1e-05


def shifted(value, axis, steps):
    count = lax.axis_size(axis)
    pairs = [(source, (source + steps) % count) for source in range(count)]
    return lax.ppermute(value, axis, pairs)


def capped(raw_score):
    return cap_limit * jnp.tanh(raw_score / cap_limit)


def layer_norm(rows_in, gain_row):
    widened = rows_in.astype(jnp.float32)
    center = widened - jnp.mean(widened, axis=-1, keepdims=True)
    spread = jnp.mean(center * center, axis=-1, keepdims=True)
    return (center * lax.rsqrt(spread + epsilon) * gain_row).astype(jnp.bfloat16)


def edge_counts(index_rows, block_rows):
    columns = jnp.arange(block_rows, dtype=jnp.int32)
    return jnp.sum((index_rows[..., None] == columns).astype(jnp.float32), axis=0)


def pair_terms(query_rows, pair_rows, counts, heads_count, scale_factor):
    batch_count, block_rows, model_width = query_rows.shape
    head_width = model_width // heads_count
    query_heads = query_rows.reshape(batch_count, block_rows, heads_count, head_width)
    key_heads = pair_rows[:, :, :model_width].reshape(
        batch_count, block_rows, heads_count, head_width
    )
    value_heads = pair_rows[:, :, model_width:].reshape(
        batch_count, block_rows, heads_count, head_width
    )
    raw_score = (
        jnp.einsum("nqhd,nkhd->nhqk", query_heads, key_heads, preferred_element_type=jnp.float32)
        * scale_factor
    )
    weights = (counts[:, None] * jnp.exp(capped(raw_score))).astype(jnp.bfloat16)
    numerator = jnp.einsum(
        "nhqk,nkhd->nqhd", weights, value_heads, preferred_element_type=jnp.float32
    )
    denominator = jnp.swapaxes(jnp.sum(weights.astype(jnp.float32), axis=3), 1, 2)
    return (numerator, denominator)


def body(
    activations,
    norm_gain,
    project_in,
    project_out,
    virtual_keys,
    virtual_id,
    local_rows,
    slot_block,
    slot_count,
    slot_rows,
):
    rows_here = activations.shape[1]
    model_width = activations.shape[2]
    block_rows = slot_rows.shape[3]
    blocks_here = rows_here // block_rows
    slots_per = slot_block.shape[1]
    heads_count = HEADS
    head_width = model_width // heads_count
    scale_factor = head_width ** (-0.5)
    devices_node = lax.axis_size("node")
    virtual_count = virtual_keys.shape[1]
    normed = layer_norm(activations[0], norm_gain[0])
    projected = jnp.dot(normed, project_in[0], preferred_element_type=jnp.float32)
    queries = projected[:, :model_width].astype(jnp.bfloat16)
    key_value = projected[:, model_width:].astype(jnp.bfloat16)
    source_device = slot_block // blocks_here
    source_local = slot_block % blocks_here
    slot_live = jnp.arange(slots_per, dtype=jnp.int32)[None, :] < slot_count[:, None]
    peer_ids = jnp.arange(devices_node, dtype=jnp.int32)
    matches = (source_device[:, :, None] == peer_ids) & slot_live[:, :, None]
    wanted = jnp.max(jnp.where(matches, source_local[:, :, None], 0), axis=(0, 1))
    asked = lax.all_to_all(
        wanted.reshape(devices_node, 1), "node", split_axis=0, concat_axis=0, tiled=True
    )
    outgoing = jnp.take(normed.reshape(blocks_here, block_rows, model_width), asked[:, 0], axis=0)
    arrived = lax.all_to_all(outgoing, "node", split_axis=0, concat_axis=0, tiled=True)
    weight_pair = project_in[0][:, model_width:]
    member = (
        virtual_id[:, 0][:, None] == jnp.arange(virtual_count, dtype=jnp.int32)[None, :]
    ).astype(jnp.float32)
    own_key = jnp.dot(member, virtual_keys[0].astype(jnp.float32), precision=lax.Precision.HIGHEST)
    keys_wide = key_value[:, :model_width].astype(jnp.float32)
    pool_raw = (
        jnp.sum((own_key * keys_wide).reshape(rows_here, heads_count, head_width), axis=2)
        * scale_factor
    )
    pool_weight = jnp.exp(capped(pool_raw)).astype(jnp.bfloat16)
    weighted = pool_weight.astype(jnp.float32)[:, :, None] * key_value[:, model_width:].astype(
        jnp.float32
    ).reshape(rows_here, heads_count, head_width)
    pool_num = jnp.einsum("rj,rhd->jhd", member, weighted, precision=lax.Precision.HIGHEST)
    pool_den = jnp.dot(member.T, pool_weight.astype(jnp.float32), precision=lax.Precision.HIGHEST)
    pool_num, pool_den = lax.psum((pool_num, pool_den), "node")
    pooled = pool_num / pool_den[:, :, None]
    query_blocks = queries.reshape(blocks_here, block_rows, model_width)
    local_counts = edge_counts(
        local_rows.reshape(local_rows.shape[0], blocks_here, block_rows), block_rows
    )
    numerator, denominator = pair_terms(
        query_blocks,
        key_value.reshape(blocks_here, block_rows, 2 * model_width),
        local_counts,
        heads_count,
        scale_factor,
    )
    for slot_index in range(slots_per):
        counts_now = edge_counts(jnp.moveaxis(slot_rows[:, slot_index], 1, 0), block_rows)
        counts_now = counts_now * slot_live[:, slot_index].astype(jnp.float32)[:, None, None]
        picked = jnp.take(arrived, source_device[:, slot_index], axis=0)
        flat_states = picked.reshape(-1, model_width)
        rebuilt = jnp.dot(flat_states, weight_pair, preferred_element_type=jnp.float32)
        extra_num, extra_den = pair_terms(
            query_blocks,
            rebuilt.astype(jnp.bfloat16).reshape(picked.shape[0], block_rows, 2 * model_width),
            counts_now,
            heads_count,
            scale_factor,
        )
        numerator = numerator + extra_num
        denominator = denominator + extra_den
    attended = (numerator / denominator[..., None]).reshape(rows_here, model_width)
    broadcast_pool = jnp.dot(
        member, pooled.reshape(virtual_count, model_width), precision=lax.Precision.HIGHEST
    )
    mixed = (attended + broadcast_pool).astype(jnp.bfloat16)
    updated = (
        activations[0].astype(jnp.float32)
        + jnp.dot(mixed, project_out[0], preferred_element_type=jnp.float32)
    ).astype(jnp.bfloat16)
    return shifted(updated[None], "segment", 1)


def solution(mesh):
    placed = (
        P("segment", "node", None),
        P("segment", None),
        P("segment", None, None),
        P("segment", None, None),
        P("segment", None, None),
        P("node", None),
        P(None, "node"),
        P("node", None),
        P("node"),
        P("node", None, None, None),
    )
    return jax.shard_map(
        body, mesh=mesh, in_specs=placed, out_specs=P("segment", "node", None), check_vma=False
    )
```

profile of v0, /device:TPU:0, one launch (start us, length us, event | category | flops | bytes accessed | tf_op | source)
XLA Modules:
  0.0 160.3 jit_solution(8969686221533247456)
XLA Ops:
  2.3 6.3 %all-to-all-start = ((s32[8,1,1]{2,1,0:T(1,128)}), s32[8,1,1]{2,1,0:T(1,128)S(1)}, u32[]{:S(2)}, u32[]{:S(2)}) async-start(s32[8,1,1]{2,1,0:T(1,128)} %copy.222), calls=%async_computation | async-start | bytes 8192 | tf_op jit(solution)/shard_map/all_to_all | solution.py:89
  10.8 2.1 %convolution_convert_fusion = bf16[256,1536]{1,0:T(8,128)(2,1)S(1)} fusion(bf16[1,256,512]{2,1,0:T(8,128)(2,1)} %param.12, f32[512]{0:T(512)} %bitcast.218, f32[256]{0:T(256)S(1)} %get-tuple-element.57, f32[256]{0:T(256)S(1)} %get-tuple-element.55, bf16[1,512,1536]{2,1,0:T(8,128)(2,1)} %param.14), kind=kOutput, calls=%fused_computation.9 | convolution fusion | flops 403701760 | bytes 2625536 | tf_op jit(solution)/shard_map/dot_general | solution.py:80
  26.6 29.3 %all-reduce = (f32[4,8,64]{2,0,1:T(4,128)S(1)}, f32[4,8]{1,0:T(4,128)S(1)}) all-reduce(f32[4,8,64]{2,0,1:T(4,128)S(1)} %fusion.53, f32[4,8]{1,0:T(4,128)S(1)} %fusion.71), channel_id=1, replica_groups=mesh['segment'=4,'node'=8] {'node'}, use_global_device_ids=true, to_apply=%region_22.24 | all-reduce | flops 2080 | bytes 16640 | tf_op jit(solution)/shard_map/psum | solution.py:110
  58.4 3.7 %all-to-all-start.1 = ((bf16[8,128,512]{2,1,0:T(8,128)(2,1)}), bf16[8,128,512]{2,1,0:T(8,128)(2,1)S(1)}, u32[]{:S(2)}, u32[]{:S(2)}) async-start(bf16[8,128,512]{2,1,0:T(8,128)(2,1)} %broadcast_select_fusion), calls=%async_computation.1 | async-start | bytes 2097152 | tf_op jit(solution)/shard_map/all_to_all | solution.py:93
  66.4 22.1 %all-to-all-done.1 = bf16[8,128,512]{2,1,0:T(8,128)(2,1)S(1)} async-done(((bf16[8,128,512]{2,1,0:T(8,128)(2,1)}), bf16[8,128,512]{2,1,0:T(8,128)(2,1)S(1)}, u32[]{:S(2)}, u32[]{:S(2)}) %all-to-all-start.1) | async-done | bytes 1048608 | tf_op jit(solution)/shard_map/all_to_all | solution.py:93
  89.2 1.7 %convolution_convert_fusion.8 = bf16[256,1024]{1,0:T(8,128)(2,1)S(1)} fusion(bf16[256,512]{1,0:T(8,128)(2,1)S(1)} %bitcast.196, bf16[512,1536]{1,0:T(8,128)(2,1)} %bitcast.221), kind=kOutput, calls=%fused_computation.64 | convolution fusion | flops 268697600 | bytes 1835008 | tf_op jit(solution)/shard_map/dot_general | solution.py:128
  92.6 1.7 %convolution_convert_fusion.7 = bf16[256,1024]{1,0:T(8,128)(2,1)S(1)} fusion(bf16[256,512]{1,0:T(8,128)(2,1)S(1)} %bitcast.197, bf16[512,1536]{1,0:T(8,128)(2,1)} %bitcast.222), kind=kOutput, calls=%fused_computation.63 | convolution fusion | flops 268697600 | bytes 1835008 | tf_op jit(solution)/shard_map/dot_general | solution.py:128
  96.7 1.7 %convolution_convert_fusion.6 = bf16[256,1024]{1,0:T(8,128)(2,1)S(1)} fusion(bf16[256,512]{1,0:T(8,128)(2,1)S(1)} %bitcast.198, bf16[512,1536]{1,0:T(8,128)(2,1)} %bitcast.223), kind=kOutput, calls=%fused_computation.62 | convolution fusion | flops 268697600 | bytes 1835008 | tf_op jit(solution)/shard_map/dot_general | solution.py:128
  102.5 1.7 %convolution_convert_fusion.5 = bf16[256,1024]{1,0:T(8,128)(2,1)S(1)} fusion(bf16[256,512]{1,0:T(8,128)(2,1)S(1)} %bitcast.199, bf16[512,1536]{1,0:T(8,128)(2,1)} %bitcast.224), kind=kOutput, calls=%fused_computation.61 | convolution fusion | flops 268697600 | bytes 1835008 | tf_op jit(solution)/shard_map/dot_general | solution.py:128
  106.1 1.8 %copy.244 = bf16[2,128,512]{1,2,0:T(8,128)(2,1)} copy(bf16[2,128,512]{2,1,0:T(8,128)(2,1)} %get-tuple-element.26) | data formatting | bytes 524288 | tf_op jit(solution)/shard_map/slice | solution.py:39
  110.3 1.7 %convolution_convert_fusion.4 = bf16[256,1024]{1,0:T(8,128)(2,1)S(1)} fusion(bf16[256,512]{1,0:T(8,128)(2,1)S(1)} %bitcast.200, bf16[512,1536]{1,0:T(8,128)(2,1)} %bitcast.225), kind=kOutput, calls=%fused_computation.60 | convolution fusion | flops 268697600 | bytes 1835008 | tf_op jit(solution)/shard_map/dot_general | solution.py:128
  112.8 1.8 %copy.247 = bf16[2,128,512]{1,2,0:T(8,128)(2,1)} copy(bf16[2,128,512]{2,1,0:T(8,128)(2,1)} %get-tuple-element.25) | data formatting | bytes 524288 | tf_op jit(solution)/shard_map/slice | solution.py:42
  114.6 1.8 %copy.250 = bf16[2,128,512]{1,2,0:T(8,128)(2,1)} copy(bf16[2,128,512]{2,1,0:T(8,128)(2,1)} %get-tuple-element.24) | data formatting | bytes 524288 | tf_op jit(solution)/shard_map/slice | solution.py:39
  118.9 1.7 %convolution_convert_fusion.3 = bf16[256,1024]{1,0:T(8,128)(2,1)S(1)} fusion(bf16[256,512]{1,0:T(8,128)(2,1)S(1)} %bitcast.201, bf16[512,1536]{1,0:T(8,128)(2,1)} %bitcast.226), kind=kOutput, calls=%fused_computation.59 | convolution fusion | flops 268697600 | bytes 1835008 | tf_op jit(solution)/shard_map/dot_general | solution.py:128
  121.4 1.8 %copy.253 = bf16[2,128,512]{1,2,0:T(8,128)(2,1)} copy(bf16[2,128,512]{2,1,0:T(8,128)(2,1)} %get-tuple-element.23) | data formatting | bytes 524288 | tf_op jit(solution)/shard_map/slice | solution.py:42
  123.2 1.8 %copy.256 = bf16[2,128,512]{1,2,0:T(8,128)(2,1)} copy(bf16[2,128,512]{2,1,0:T(8,128)(2,1)} %get-tuple-element.22) | data formatting | bytes 524288 | tf_op jit(solution)/shard_map/slice | solution.py:39
  127.4 1.7 %convolution_convert_fusion.2 = bf16[256,1024]{1,0:T(8,128)(2,1)S(1)} fusion(bf16[256,512]{1,0:T(8,128)(2,1)S(1)} %bitcast.202, bf16[512,1536]{1,0:T(8,128)(2,1)} %bitcast.227), kind=kOutput, calls=%fused_computation.58 | convolution fusion | flops 268697600 | bytes 1835008 | tf_op jit(solution)/shard_map/dot_general | solution.py:128
  130.0 1.8 %copy.259 = bf16[2,128,512]{1,2,0:T(8,128)(2,1)} copy(bf16[2,128,512]{2,1,0:T(8,128)(2,1)} %get-tuple-element.21) | data formatting | bytes 524288 | tf_op jit(solution)/shard_map/slice | solution.py:42
  131.8 1.8 %copy.262 = bf16[2,128,512]{1,2,0:T(8,128)(2,1)} copy(bf16[2,128,512]{2,1,0:T(8,128)(2,1)} %get-tuple-element.20) | data formatting | bytes 524288 | tf_op jit(solution)/shard_map/slice | solution.py:39
  136.0 1.7 %convolution_convert_fusion.1 = bf16[256,1024]{1,0:T(8,128)(2,1)S(1)} fusion(bf16[256,512]{1,0:T(8,128)(2,1)S(1)} %bitcast.203, bf16[512,1536]{1,0:T(8,128)(2,1)} %bitcast.228), kind=kOutput, calls=%fused_computation.57 | convolution fusion | flops 268697600 | bytes 1835008 | tf_op jit(solution)/shard_map/dot_general | solution.py:128
  139.4 1.6 %convert_reduce_fusion.8 = (f32[2,8,128]{2,1,0:T(8,128)S(1)}, bf16[2,8,128,128]{2,3,1,0:T(8,128)(2,1)S(1)}) fusion(bf16[2,128,8,64]{1,3,2,0:T(8,128)(2,1)} %copy-done.5, bf16[2,128,8,64]{1,3,2,0:T(8,128)(2,1)} %bitcast.205, f32[2,128,128]{1,2,0:T(8,128)S(1)} %copy.225), kind=kOutput, calls=%fused_computation.97 | convolution fusion | flops 35125248 | bytes 1187840 | tf_op jit(solution)/shard_map/nqhd,nkhd->nhqk/dot_general | solution.py:46
  141.1 1.6 %convert_reduce_fusion.7 = (f32[2,8,128]{2,1,0:T(8,128)S(1)}, bf16[2,8,128,128]{2,3,1,0:T(8,128)(2,1)S(1)}) fusion(bf16[2,128,8,64]{1,3,2,0:T(8,128)(2,1)} %copy-done.5, bf16[2,128,8,64]{1,3,2,0:T(8,128)(2,1)} %bitcast.206, f32[2,128,128]{1,2,0:T(8,128)} %copy.231), kind=kOutput, calls=%fused_computation.96 | convolution fusion | flops 35125248 | bytes 1187840 | tf_op jit(solution)/shard_map/nqhd,nkhd->nhqk/dot_general | solution.py:46
  150.8 1.5 collective-permute-start
  152.3 7.3 %collective-permute-done = bf16[1,256,512]{2,1,0:T(8,128)(2,1)S(1)} collective-permute-done((bf16[1,256,512]{2,1,0:T(8,128)(2,1)S(1)}, bf16[1,256,512]{2,1,0:T(8,128)(2,1)S(1)}, u32[]{:S(2)}, u32[]{:S(2)}) %collective-permute-start) | collective-permute-done | bytes 262176 | tf_op jit(solution)/shard_map/ppermute | solution.py:16
  (202 shorter events, 57.6 us)
Async XLA Ops:
  0.0 150.5 %copy-start = (bf16[1,512,512]{2,1,0:T(8,128)(2,1)S(1)}, bf16[1,512,512]{2,1,0:T(8,128)(2,1)}, u32[]{:S(2)}) copy-start(bf16[1,512,512]{2,1,0:T(8,128)(2,1)} %param.15) | copy-start | bytes 1572868
  2.3 54.1 %all-to-all-start = ((s32[8,1,1]{2,1,0:T(1,128)}), s32[8,1,1]{2,1,0:T(1,128)S(1)}, u32[]{:S(2)}, u32[]{:S(2)}) async-start(s32[8,1,1]{2,1,0:T(1,128)} %copy.222), calls=%async_computation | async-start | bytes 8192 | tf_op jit(solution)/shard_map/all_to_all | solution.py:89
  14.8 1.9 %copy-start.20 = (s32[2,8,4,128]{3,2,1,0:T(4,128)S(1)}, s32[2,8,4,128]{3,2,1,0:T(4,128)}, u32[]{:S(2)}) copy-start(s32[2,8,4,128]{3,2,1,0:T(4,128)} %param.21) | copy-start | bytes 98308
  15.2 3.9 %copy-start.30 = (f32[2]{0:T(128)S(1)}, f32[2]{0:T(128)}, u32[]{:S(2)}) copy-start(f32[2]{0:T(128)} %get-tuple-element.49) | copy-start | bytes 28
  15.6 49.5 %copy-start.5 = (bf16[2,128,8,64]{1,3,2,0:T(8,128)(2,1)}, bf16[2,128,8,64]{1,3,2,0:T(8,128)(2,1)S(1)}, u32[]{:S(2)}) copy-start(bf16[2,128,8,64]{1,3,2,0:T(8,128)(2,1)S(1)} %copy.219) | copy-start | bytes 786436
  16.6 5.1 %copy-start.29 = (f32[2]{0:T(128)S(1)}, f32[2]{0:T(128)}, u32[]{:S(2)}) copy-start(f32[2]{0:T(128)} %get-tuple-element.47) | copy-start | bytes 28
  23.9 32.2 %copy-start.1 = (bf16[1,256,512]{2,1,0:T(8,128)(2,1)S(1)}, bf16[1,256,512]{2,1,0:T(8,128)(2,1)}, u32[]{:S(2)}) copy-start(bf16[1,256,512]{2,1,0:T(8,128)(2,1)} %param.12) | copy-start | bytes 786436
  23.9 32.2 %copy-start.25 = (f32[1,512]{1,0:T(1,128)S(1)}, f32[1,512]{1,0:T(1,128)}, u32[]{:S(2)}) copy-start(f32[1,512]{1,0:T(1,128)} %param.13) | copy-start | bytes 6148
  58.4 30.1 %all-to-all-start.1 = ((bf16[8,128,512]{2,1,0:T(8,128)(2,1)}), bf16[8,128,512]{2,1,0:T(8,128)(2,1)S(1)}, u32[]{:S(2)}, u32[]{:S(2)}) async-start(bf16[8,128,512]{2,1,0:T(8,128)(2,1)} %broadcast_select_fusion), calls=%async_computation.1 | async-start | bytes 2097152 | tf_op jit(solution)/shard_map/all_to_all | solution.py:93
  111.9 5.9 %copy-start.28 = (pred[2]{0:T(512)(128)(4,1)S(1)}, pred[2]{0:T(512)(128)(4,1)}, u32[]{:S(2)}) copy-start(pred[2]{0:T(512)(128)(4,1)} %get-tuple-element.86) | copy-start | bytes 10
  120.5 5.9 %copy-start.27 = (pred[2]{0:T(512)(128)(4,1)S(1)}, pred[2]{0:T(512)(128)(4,1)}, u32[]{:S(2)}) copy-start(pred[2]{0:T(512)(128)(4,1)} %get-tuple-element.85) | copy-start | bytes 10
  129.1 5.9 %copy-start.26 = (pred[2]{0:T(512)(128)(4,1)S(1)}, pred[2]{0:T(512)(128)(4,1)}, u32[]{:S(2)}) copy-start(pred[2]{0:T(512)(128)(4,1)} %get-tuple-element.84) | copy-start | bytes 10
  139.4 3.3 %copy-start.6 = (bf16[2,128,8,64]{1,3,2,0:T(8,128)(2,1)S(1)}, bf16[2,128,8,64]{1,3,2,0:T(8,128)(2,1)}, u32[]{:S(2)}) copy-start(bf16[2,128,8,64]{1,3,2,0:T(8,128)(2,1)} %copy-done.5) | copy-start | bytes 786436
  139.4 3.3 %copy-start.7 = (bf16[2,128,512]{1,2,0:T(8,128)(2,1)S(1)}, bf16[2,128,512]{1,2,0:T(8,128)(2,1)}, u32[]{:S(2)}) copy-start(bf16[2,128,512]{1,2,0:T(8,128)(2,1)} %copy.238) | copy-start | bytes 786436
  139.4 3.3 %copy-start.14 = (f32[2,128,128]{1,2,0:T(8,128)S(1)}, f32[2,128,128]{1,2,0:T(8,128)}, u32[]{:S(2)}) copy-start(f32[2,128,128]{1,2,0:T(8,128)} %copy.237) | copy-start | bytes 393220
  141.1 2.3 %copy-start.9 = (bf16[2,128,512]{1,2,0:T(8,128)(2,1)S(1)}, bf16[2,128,512]{1,2,0:T(8,128)(2,1)}, u32[]{:S(2)}) copy-start(bf16[2,128,512]{1,2,0:T(8,128)(2,1)} %copy.244) | copy-start | bytes 786436
  141.1 2.3 %copy-start.15 = (f32[2,128,128]{1,2,0:T(8,128)S(1)}, f32[2,128,128]{1,2,0:T(8,128)}, u32[]{:S(2)}) copy-start(f32[2,128,128]{1,2,0:T(8,128)} %copy.243) | copy-start | bytes 393220
  142.8 1.2 copy-start.10
  142.8 1.2 copy-start.16
  143.4 1.2 copy-start.11
  143.4 1.2 copy-start.17
  144.0 1.2 copy-start.12
  144.0 1.2 copy-start.19
  150.8 8.8 %collective-permute-start = (bf16[1,256,512]{2,1,0:T(8,128)(2,1)S(1)}, bf16[1,256,512]{2,1,0:T(8,128)(2,1)S(1)}, u32[]{:S(2)}, u32[]{:S(2)}) collective-permute-start(bf16[1,256,512]{2,1,0:T(8,128)(2,1)S(1)} %fusion.49), channel_id=1, source_target_pairs={{0,8},{8,16},{16,24},{24,0},{1,9},{9,17},{17,25},{25,1},{2,10},{10... | collective-permute-start | bytes 786440 | tf_op jit(solution)/shard_map/ppermute | solution.py:16
  (10 other events, 10.1 us)
where the time goes:
time: 161 us; the launch traced here: 160 us
  local copies, waits for them, and re-layouts  42.7 us (27%)
  blocking collectives  29.3 us (18%)
  waiting for transfers between devices  29.3 us (18%)
  matrix products  27.2 us (17%)
  other arithmetic  19.1 us (12%)
  starting transfers between devices  11.6 us (7%)
    psum x1, blocking collectives, body(): pool_num, pool_den = lax.psum((pool_num, pool_den), 'node')  29.3 us
    all_to_all x1, waiting for transfers between devices, body(): lax.all_to_all(outgoing, 'node', split_axis=0, concat_axis=0, tiled=True)  22.1 us
    slice x18, local copies, waits for them, and re-layouts, pair_terms(): pair_rows[:, :, :model_width]  15.1 us
    dot_general x8, matrix products, body(): jnp.dot(flat_states, weight_pair, preferred_element_type=jnp.float32)  13.3 us
    slice x9, local copies, waits for them, and re-layouts, pair_terms(): pair_rows[:, :, model_width:]  8.99 us
    gather x8, local copies, waits for them, and re-layouts, body(): picked = jnp.take(arrived, source_device[:, slot_index], axis=0)  7.96 us
    dot_general x9, matrix products, pair_terms(): jnp.einsum('nqhd,nkhd->nhqk', query_heads, key_heads, preferred_element_t...  7.67 us
    ppermute x1, waiting for transfers between devices, shifted(): return lax.ppermute(value, axis, pairs)  7.25 us
  transfers between devices with their start and end apart: 3, of which 2 were waited for; matrix products, arithmetic and copies ran while one was open for 14% of the time, Pallas kernels for 0%

commit v1 on v0

v1 whole, which is shorter than its diff:
```python
import functools

import jax
import jax.numpy as jnp
from jax import lax
from jax.experimental import pallas as pl
from jax.experimental.pallas import tpu as pltpu
from jax.sharding import PartitionSpec as P

HEADS = 8
EPSILON = 1e-05
CAP_LIMIT = 10.0
LOG2E = 1.4426950408889634
ONES_ROWS = 16
F32 = jnp.float32
BF16 = jnp.bfloat16
VMEM = pl.BlockSpec(memory_space=pltpu.VMEM)
SMEM = pl.BlockSpec(memory_space=pltpu.SMEM)


def shifted(value, axis, steps):
    count = lax.axis_size(axis)
    pairs = [(source, (source + steps) % count) for source in range(count)]
    return lax.ppermute(value, axis, pairs)


def norm_rows(rows_in, gain_row):
    widened = rows_in.astype(F32)
    center = widened - jnp.mean(widened, axis=-1, keepdims=True)
    spread = jnp.mean(center * center, axis=-1, keepdims=True)
    return (center * lax.rsqrt(spread + EPSILON) * gain_row).astype(BF16)


def exp_capped(raw, scale):
    return jnp.exp2((CAP_LIMIT * LOG2E) * jnp.tanh(raw * (scale / CAP_LIMIT)))


def counts_of(index_rows, block_rows):
    rows = lax.broadcasted_iota(jnp.int32, (block_rows, index_rows.shape[1]), 0)
    total = jnp.zeros(rows.shape, F32)
    for j in range(index_rows.shape[0]):
        total = total + jnp.where(index_rows[j : j + 1, :] == rows, 1.0, 0.0)
    return total


def mm(a, b):
    return jnp.dot(a, b, preferred_element_type=F32)


def mm_nt(a, b):
    return lax.dot_general(a, b, (((1,), (1,)), ((), ())), preferred_element_type=F32)


def mm_tn(a, b):
    return lax.dot_general(a, b, (((0,), (0,)), ((), ())), preferred_element_type=F32)


def local_kernel(
    x_ref, gain_ref, win_ref, vk_ref, vid_ref, lrows_ref,
    qbd_ref, num_ref, den_ref, pool_ref, wvt_ref,
):
    rows, width = x_ref.shape
    blocks, pairs, wide, _ = qbd_ref.shape
    br = rows // blocks
    head = width // HEADS
    scale = head ** (-0.5)
    virtual = vk_ref.shape[0]
    normed = norm_rows(x_ref[...], gain_ref[...])
    q = mm(normed, win_ref[:, :width]).astype(BF16)
    k = mm(normed, win_ref[:, width : 2 * width]).astype(BF16)
    v = mm(normed, win_ref[:, 2 * width :]).astype(BF16)
    qt = q.T
    vt = v.T
    wvt_ref[...] = win_ref[:, 2 * width :].T
    zero = jnp.zeros((head, br), BF16)
    ones = jnp.ones((ONES_ROWS, br), BF16)

    head_of_lane = lax.broadcasted_iota(jnp.int32, (HEADS, width), 1) // head
    head_of_row = lax.broadcasted_iota(jnp.int32, (HEADS, width), 0)
    own_head = head_of_lane == head_of_row
    vkf = vk_ref[...].astype(F32)
    vkbd = jnp.concatenate(
        [
            jnp.where(own_head, jnp.broadcast_to(vkf[j : j + 1, :], (HEADS, width)), 0.0)
            for j in range(virtual)
        ],
        axis=0,
    ).astype(BF16)
    raw = mm_nt(k, vkbd)
    lanes = lax.broadcasted_iota(jnp.int32, raw.shape, 1) // HEADS
    pool_w = jnp.where(vid_ref[...] == lanes, exp_capped(raw, scale), 0.0).astype(BF16)
    pool_num = mm_tn(pool_w, v)
    pool_den = mm_tn(pool_w, jnp.ones((rows, width), BF16))
    for j in range(virtual):
        part = slice(j * HEADS, (j + 1) * HEADS)
        pool_ref[j : j + 1, :] = jnp.sum(
            jnp.where(own_head, pool_num[part], 0.0), axis=0, keepdims=True
        )
        pool_ref[virtual + j : virtual + j + 1, :] = jnp.sum(
            jnp.where(own_head, pool_den[part], 0.0), axis=0, keepdims=True
        )

    for b in range(blocks):
        cols = slice(b * br, (b + 1) * br)
        counts = counts_of(lrows_ref[:, cols], br)
        counts2 = jnp.concatenate([counts, counts], axis=1)
        for t in range(pairs):
            r0 = t * wide
            mid = r0 + head
            end = r0 + wide
            bd = jnp.concatenate(
                [
                    jnp.concatenate([qt[r0:mid, cols], zero], axis=1),
                    jnp.concatenate([zero, qt[mid:end, cols]], axis=1),
                ],
                axis=0,
            )
            qbd_ref[b, t] = bd
            p = (counts2 * exp_capped(mm(k[cols, r0:end], bd), scale)).astype(BF16)
            o = mm(jnp.concatenate([vt[r0:end, cols], ones], axis=0), p)
            num_ref[b, r0:mid, :] = o[:head, :br]
            num_ref[b, mid:end, :] = o[head:wide, br:]
            den_ref[b, 2 * t : 2 * t + 1, :] = o[wide : wide + 1, :br]
            den_ref[b, 2 * t + 1 : 2 * t + 2, :] = o[wide : wide + 1, br:]


def slot_kernel(
    sblock_ref, scount_ref, xg_ref, gain_ref, win_ref, wvt_ref, srows_ref,
    qbd_ref, num_ref, den_ref, pool_ref, vid_ref, x_ref, wo_ref,
    out_ref, k_scr, vt_scr, num_scr, den_scr, want_ref,
):
    peers = xg_ref.shape[0]
    rows, width = x_ref.shape
    blocks, pairs, wide, _ = qbd_ref.shape
    br = rows // blocks
    head = width // HEADS
    scale = head ** (-0.5)
    virtual = pool_ref.shape[1] // 2
    slots = sblock_ref.shape[1]

    for d in range(peers):
        want_ref[d] = 0
    for b in range(blocks):
        for e in range(slots):
            entry = sblock_ref[b, e]
            want_ref[entry // blocks] = entry % blocks
    ones = jnp.ones((ONES_ROWS, br), BF16)

    def project(c, carry):
        d0 = 2 * c
        d1 = 2 * c + 1
        w0 = pl.multiple_of(want_ref[d0] * br, br)
        w1 = pl.multiple_of(want_ref[d1] * br, br)
        xs = jnp.concatenate([xg_ref[d0, pl.ds(w0, br), :], xg_ref[d1, pl.ds(w1, br), :]], axis=0)
        normed = norm_rows(xs, gain_ref[...])
        k = mm(normed, win_ref[:, width : 2 * width]).astype(BF16)
        vt = mm_nt(wvt_ref[...], normed).astype(BF16)
        k_scr[d0] = k[:br]
        k_scr[d1] = k[br:]
        for t in range(pairs):
            part = slice(t * wide, (t + 1) * wide)
            vt_scr[d0, t, :wide, :] = vt[part, :br]
            vt_scr[d1, t, :wide, :] = vt[part, br:]
            vt_scr[d0, t, wide:, :] = ones
            vt_scr[d1, t, wide:, :] = ones
        return carry

    lax.fori_loop(0, peers // 2, project, 0, unroll=peers <= 8)

    num_scr[...] = num_ref[...]
    den_scr[...] = den_ref[...]
    for b in range(blocks):
        live = scount_ref[b]

        def two_slots(i, carry, b=b, live=live):
            e0 = 2 * i
            e1 = e0 + 1
            d0 = sblock_ref[b, e0] // blocks
            d1 = sblock_ref[b, e1] // blocks
            flag = jnp.where(e1 < live, 1.0, 0.0).astype(F32)
            c0 = counts_of(srows_ref[b, e0], br)
            c1 = counts_of(srows_ref[b, e1], br) * flag
            counts = jnp.concatenate([c0, c1], axis=0)
            counts2 = jnp.concatenate([counts, counts], axis=1)
            for t in range(pairs):
                r0 = t * wide
                mid = r0 + head
                end = r0 + wide
                keys = jnp.concatenate([k_scr[d0, :, r0:end], k_scr[d1, :, r0:end]], axis=0)
                p = (counts2 * exp_capped(mm(keys, qbd_ref[b, t]), scale)).astype(BF16)
                o = mm(jnp.concatenate([vt_scr[d0, t], vt_scr[d1, t]], axis=1), p)
                num_scr[b, r0:mid, :] += o[:head, :br]
                num_scr[b, mid:end, :] += o[head:wide, br:]
                den_scr[b, 2 * t : 2 * t + 1, :] += o[wide : wide + 1, :br]
                den_scr[b, 2 * t + 1 : 2 * t + 2, :] += o[wide : wide + 1, br:]
            return carry

        lax.fori_loop(0, (live + 1) // 2, two_slots, 0)

    total = pool_ref[0]
    for d in range(1, peers):
        total = total + pool_ref[d]
    pooled = total[:virtual] / total[virtual:]
    vid = vid_ref[...]
    spread = jnp.broadcast_to(pooled[0:1, :], (rows, width))
    for j in range(1, virtual):
        spread = jnp.where(vid == j, pooled[j : j + 1, :], spread)
    for b in range(blocks):
        part = slice(b * br, (b + 1) * br)
        att = jnp.concatenate(
            [
                num_scr[b, h * head : (h + 1) * head, :] / den_scr[b, h : h + 1, :]
                for h in range(HEADS)
            ],
            axis=0,
        )
        mixed = (att.T + spread[part]).astype(BF16)
        out_ref[part, :] = (x_ref[part, :].astype(F32) + mm(mixed, wo_ref[...])).astype(BF16)


def body(
    activations,
    norm_gain,
    project_in,
    project_out,
    virtual_keys,
    virtual_id,
    local_rows,
    slot_block,
    slot_count,
    slot_rows,
):
    _, rows, width = activations.shape
    br = slot_rows.shape[3]
    blocks = rows // br
    peers = lax.axis_size("node")
    virtual = virtual_keys.shape[1]
    pairs = HEADS // 2
    wide = width // pairs
    x = activations[0]
    gathered = lax.all_gather(x, "node", axis=0, tiled=False)
    qbd, num, den, pool, wvt = pl.pallas_call(
        local_kernel,
        out_shape=(
            jax.ShapeDtypeStruct((blocks, pairs, wide, 2 * br), BF16),
            jax.ShapeDtypeStruct((blocks, width, br), F32),
            jax.ShapeDtypeStruct((blocks, HEADS, br), F32),
            jax.ShapeDtypeStruct((2 * virtual, width), F32),
            jax.ShapeDtypeStruct((width, width), BF16),
        ),
        in_specs=[VMEM] * 6,
        out_specs=[VMEM] * 5,
        compiler_params=pltpu.CompilerParams(vmem_limit_bytes=40 * 2**20),
        cost_estimate=pl.CostEstimate(
            flops=2 * rows * width * 4 * width, bytes_accessed=4 * 2**20, transcendentals=2**20
        ),
        name="own_rows",
    )(x, norm_gain, project_in[0], virtual_keys[0], virtual_id, local_rows)
    pools = lax.all_to_all(
        jnp.broadcast_to(pool[None], (peers,) + pool.shape), "node", split_axis=0, concat_axis=0, tiled=True
    )
    updated = pl.pallas_call(
        slot_kernel,
        out_shape=jax.ShapeDtypeStruct((rows, width), BF16),
        in_specs=[SMEM, SMEM] + [VMEM] * 12,
        out_specs=VMEM,
        scratch_shapes=[
            pltpu.VMEM((peers, br, width), BF16),
            pltpu.VMEM((peers, pairs, wide + ONES_ROWS, br), BF16),
            pltpu.VMEM((blocks, width, br), F32),
            pltpu.VMEM((blocks, HEADS, br), F32),
            pltpu.SMEM((peers,), jnp.int32),
        ],
        compiler_params=pltpu.CompilerParams(vmem_limit_bytes=48 * 2**20),
        cost_estimate=pl.CostEstimate(
            flops=2 * peers * br * width * 3 * width, bytes_accessed=6 * 2**20, transcendentals=2**22
        ),
        name="expander_slots",
    )(
        slot_block, slot_count, gathered, norm_gain, project_in[0], wvt, slot_rows,
        qbd, num, den, pools, virtual_id, x, project_out[0],
    )
    return shifted(updated[None], "segment", 1)


def solution(mesh):
    placed = (
        P("segment", "node", None),
        P("segment", None),
        P("segment", None, None),
        P("segment", None, None),
        P("segment", None, None),
        P("node", None),
        P(None, "node"),
        P("node", None),
        P("node"),
        P("node", None, None, None),
    )
    return jax.shard_map(
        body, mesh=mesh, in_specs=placed, out_specs=P("segment", "node", None), check_vma=False
    )
```

time: 161 us -> 71.3 us (0.44); the launches traced: 160 us -> 72.5 us
  local copies, waits for them, and re-layouts: 42.7 us -> 9.65 us
  matrix products: 27.2 us -> 0 us
  other arithmetic: 19.1 us -> 0 us
  blocking collectives: 29.3 us -> 16.7 us
  Pallas kernels: 0 us -> 12.5 us
  between operations: 1.03 us -> 13.5 us
  waiting for transfers between devices: 29.3 us -> 18.7 us
  starting transfers between devices: 11.6 us -> 1.56 us
    psum x1 -> x0, blocking collectives: 29.3 us -> none  [body(): pool_num, pool_den = lax.psum((pool_num, pool_den), 'node')]
    dot_general x32 -> x0, matrix products: 27.2 us -> none  [the longest x8 13.3 us: body(): jnp.dot(flat_states, weight_pair, preferred_element_type=jnp.float32)]
    slice x29 -> x0, local copies, waits for them, and re-layouts: 24.4 us -> none  [the longest x18 15.1 us: pair_terms(): pair_rows[:, :, :model_width]]
    all_to_all x2 -> x0, waiting for transfers between devices: 22.1 us -> none  [the longest x1 22.1 us: body(): lax.all_to_all(outgoing, 'node', split_axis=0, concat_axis=0, tiled=True)]
    all_to_all x0 -> x1, blocking collectives: none -> 16.7 us  [body(): lax.all_to_all(jnp.broadcast_to(pool[None], (peers,) + pool.shape), 'node...]
    pallas_call x0 -> x2, Pallas kernels: none -> 12.5 us  [the longest x1 10.3 us: body(): pl.pallas_call(slot_kernel, out_shape=jax.ShapeDtypeStruct((rows, width),...]
    all_gather x0 -> x1, waiting for transfers between devices: none -> 11.2 us  [body(): gathered = lax.all_gather(x, 'node', axis=0, tiled=False)]
    all_to_all x2 -> x0, starting transfers between devices: 10.1 us -> none  [the longest x1 6.33 us: body(): lax.all_to_all(wanted.reshape(devices_node, 1), 'node', split_axis=0, con...]
  transfers between devices with their start and end apart: 3 -> 2, of which waited for: 2 -> 2; matrix products, arithmetic and copies ran while one was open for 14% -> 1% of each run, Pallas kernels for 0% -> 3%
where the time goes in v1:
time: 71.3 us; the launch traced here: 72.5 us
  waiting for transfers between devices  18.7 us (26%)
  blocking collectives  16.7 us (23%)
  between operations  13.5 us (19%)
  Pallas kernels  12.5 us (18%)
  local copies, waits for them, and re-layouts  9.65 us (14%)
  starting transfers between devices  1.56 us (2%)
    all_to_all x1, blocking collectives, body(): lax.all_to_all(jnp.broadcast_to(pool[None], (peers,) + pool.shape), 'node...  16.7 us
    all_gather x1, waiting for transfers between devices, body(): gathered = lax.all_gather(x, 'node', axis=0, tiled=False)  11.2 us
    pallas_call x1, Pallas kernels, body(): pl.pallas_call(slot_kernel, out_shape=jax.ShapeDtypeStruct((rows, width),...  10.3 us
    unnamed x34, local copies, waits for them, and re-layouts  9.64 us
    ppermute x1, waiting for transfers between devices, shifted(): return lax.ppermute(value, axis, pairs)  6.78 us
    pallas_call x1, Pallas kernels, body(): pl.pallas_call(local_kernel, out_shape=(jax.ShapeDtypeStruct((blocks, pai...  2.14 us
    ppermute x1, starting transfers between devices, shifted(): return lax.ppermute(value, axis, pairs)  1.52 us
  transfers between devices with their start and end apart: 2, of which 2 were waited for; matrix products, arithmetic and copies ran while one was open for 1% of the time, Pallas kernels for 3%

profile of v1, /device:TPU:0, one launch (start us, length us, event | category | flops | bytes accessed | tf_op | source)
XLA Modules:
  0.0 72.5 jit_solution(8228504701258679561)
XLA Ops:
  6.5 0.0 all-gather.2.cloned.1.call-start
  6.6 0.7 all-gather.2.cloned.1.call-update
  7.3 0.8 %copy.13.vid_ref = s32[256,1]{1,0:T(8,128)S(1)} copy(s32[256,1]{0,1:T(1,128)} %param.15) | data formatting | bytes 2048 | tf_op args[5]
  8.1 0.0 copy-start
  8.1 1.4 %copy-done = bf16[1,512,1536]{2,1,0:T(8,128)(2,1)S(1)} copy-done((bf16[1,512,1536]{2,1,0:T(8,128)(2,1)S(1)}, bf16[1,512,1536]{2,1,0:T(8,128)(2,1)}, u32[]{:S(2)}) %copy-start) | copy-done | bytes 1572888
  9.5 0.9 %copy-done.2 = bf16[1,256,512]{2,1,0:T(8,128)(2,1)S(1)} copy-done((bf16[1,256,512]{2,1,0:T(8,128)(2,1)S(1)}, bf16[1,256,512]{2,1,0:T(8,128)(2,1)}, u32[]{:S(2)}) %copy-start.2) | copy-done | bytes 262168
  10.5 0.7 copy-done.4
  11.2 0.7 copy-done.5
  11.9 0.7 copy-done.6
  12.6 2.1 %own_rows.1 = (bf16[2,4,128,256]{3,2,1,0:T(8,128)(2,1)S(1)}, f32[2,512,128]{2,1,0:T(8,128)S(1)}, f32[2,8,128]{2,1,0:T(8,128)S(1)}, f32[8,512]{1,0:T(8,128)S(1)}, bf16[512,512]{1,0:T(8,128)(2,1)S(1)}) custom-call(bf16[256,512]{1,0:T(8,128)(2,1)S(1)} %bitcast.7, f32[1,512]{1,0:T(1,128)S(1)} %copy-done.6, bf16[512,1536]{1,0:T(8,128)(2,1)S(1)} %bitcast.5, ...), custom_call_target="tpu_custom_call" | custom-call | flops 536870912 | bytes 4194304 | tf_op jit(solution)/shard_map/own_rows/pallas_call | solution.py:242
  14.7 0.0 copy-start.9
  14.7 0.8 %copy-done.9 = f32[2,512,128]{2,1,0:T(8,128)} copy-done((f32[2,512,128]{2,1,0:T(8,128)}, f32[2,512,128]{2,1,0:T(8,128)S(1)}, u32[]{:S(2)}) %copy-start.9) | copy-done | bytes 524312
  15.5 0.8 %copy-done.11 = bf16[512,512]{1,0:T(8,128)(2,1)} copy-done((bf16[512,512]{1,0:T(8,128)(2,1)}, bf16[512,512]{1,0:T(8,128)(2,1)S(1)}, u32[]{:S(2)}) %copy-start.11) | copy-done | bytes 524312
  16.3 16.7 %all_to_all.5.pool_ref = f32[8,8,512]{2,1,0:T(8,128)S(1)} all-to-all(f32[8,8,512]{2,1,0:T(8,128)S(1)} %broadcast_in_dim.4), channel_id=1, replica_groups=mesh['segment'=4,'node'=8] {'node'}, dimensions={0} | all-to-all | bytes 262144 | tf_op jit(solution)/shard_map/all_to_all | solution.py:259
  33.0 11.2 %all-gather.2.cloned.1.call-done.xg_ref = bf16[8,256,512]{2,1,0:T(8,128)(2,1)} async-done(((bf16[1,256,512]{2,1,0:T(8,128)(2,1)}), bf16[8,256,512]{2,1,0:T(8,128)(2,1)}) %all-gather.2.cloned.1.call-update) | async-done | bytes 2097168 | tf_op jit(solution)/shard_map/all_gather | solution.py:241
  44.2 0.0 copy-done.3
  44.2 0.0 copy-done.7
  44.2 0.0 copy-done.13
  44.2 1.0 %copy-done.10 = f32[2,512,128]{2,1,0:T(8,128)S(1)} copy-done((f32[2,512,128]{2,1,0:T(8,128)S(1)}, f32[2,512,128]{2,1,0:T(8,128)}, u32[]{:S(2)}) %copy-start.10) | copy-done | bytes 524312
  45.3 1.0 %copy-done.12 = bf16[512,512]{1,0:T(8,128)(2,1)S(1)} copy-done((bf16[512,512]{1,0:T(8,128)(2,1)S(1)}, bf16[512,512]{1,0:T(8,128)(2,1)}, u32[]{:S(2)}) %copy-start.12) | copy-done | bytes 524312
  46.3 10.3 %expander_slots.1 = bf16[256,512]{1,0:T(8,128)(2,1)S(1)} custom-call(s32[2,8]{1,0:T(2,128)S(1)} %copy-done.14, s32[2]{0:T(128)S(1)} %copy-done.15, bf16[8,256,512]{2,1,0:T(8,128)(2,1)} %all-gather.2.cloned.1.call-done.xg_ref, f32[1,512]{1,0:T(1,128)S(1)} %copy-done.7, bf16[512,1536]{1,0:T(8,128)(2,1)S(1)} %bitcast.6, bf16[512,512]{1,0:T(8,128)(2,1)S(1)} %copy-done.12, ...), custom_call_target="tpu_custom_call" | custom-call | flops 1610612736 | bytes 6291456 | tf_op jit(solution)/shard_map/expander_slots/pallas_call | solution.py:262
  56.7 1.5 %collective-permute-start = (bf16[1,256,512]{2,1,0:T(8,128)(2,1)S(1)}, bf16[1,256,512]{2,1,0:T(8,128)(2,1)S(1)}, u32[]{:S(2)}, u32[]{:S(2)}) collective-permute-start(bf16[1,256,512]{2,1,0:T(8,128)(2,1)S(1)} %bitcast.11), channel_id=1, source_target_pairs={{0,8},{8,16},{16,24},{24,0},{1,9},{9,17},{17,25},{25,1},{2,10},{10... | collective-permute-start | bytes 786440 | tf_op jit(solution)/shard_map/ppermute | solution.py:24
  58.2 6.8 %collective-permute-done = bf16[1,256,512]{2,1,0:T(8,128)(2,1)S(1)} collective-permute-done((bf16[1,256,512]{2,1,0:T(8,128)(2,1)S(1)}, bf16[1,256,512]{2,1,0:T(8,128)(2,1)S(1)}, u32[]{:S(2)}, u32[]{:S(2)}) %collective-permute-start) | collective-permute-done | bytes 262176 | tf_op jit(solution)/shard_map/ppermute | solution.py:24
  65.0 0.7 copy.16
  (19 shorter events, 0.0 us)
Async XLA Ops:
  6.5 37.7 %copy-start.3 = (bf16[1,256,512]{2,1,0:T(8,128)(2,1)S(1)}, bf16[1,256,512]{2,1,0:T(8,128)(2,1)}, u32[]{:S(2)}) copy-start(bf16[1,256,512]{2,1,0:T(8,128)(2,1)} %param.10) | copy-start | bytes 786436
  6.5 37.7 %copy-start.7 = (f32[1,512]{1,0:T(1,128)S(1)}, f32[1,512]{1,0:T(1,128)}, u32[]{:S(2)}) copy-start(f32[1,512]{1,0:T(1,128)} %gain_ref.3) | copy-start | bytes 6148
  6.5 37.7 %copy-start.13 = (s32[2,8,4,128]{3,2,1,0:T(4,128)S(1)}, s32[2,8,4,128]{3,2,1,0:T(4,128)}, u32[]{:S(2)}) copy-start(s32[2,8,4,128]{3,2,1,0:T(4,128)} %srows_ref.1) | copy-start | bytes 98308
  6.5 37.7 %copy-start.15 = (s32[2]{0:T(128)S(1)}, s32[2]{0:T(128)}, u32[]{:S(2)}) copy-start(s32[2]{0:T(128)} %scount_ref.1) | copy-start | bytes 28
  6.5 37.7 %copy-start.14 = (s32[2,8]{1,0:T(2,128)S(1)}, s32[2,8]{1,0:T(2,128)}, u32[]{:S(2)}) copy-start(s32[2,8]{1,0:T(2,128)} %sblock_ref.1) | copy-start | bytes 196
  6.5 37.6 %all-gather.2.cloned.1.call-start = ((), (), s32[]{:S(2)}) async-start(), calls=%async_computation.1 | async-start | bytes 2359296 | tf_op jit(solution)/shard_map/all_gather | solution.py:241
  8.1 1.4 %copy-start = (bf16[1,512,1536]{2,1,0:T(8,128)(2,1)S(1)}, bf16[1,512,1536]{2,1,0:T(8,128)(2,1)}, u32[]{:S(2)}) copy-start(bf16[1,512,1536]{2,1,0:T(8,128)(2,1)} %param.12) | copy-start | bytes 4718596
  9.5 0.9 %copy-start.2 = (bf16[1,256,512]{2,1,0:T(8,128)(2,1)S(1)}, bf16[1,256,512]{2,1,0:T(8,128)(2,1)}, u32[]{:S(2)}) copy-start(bf16[1,256,512]{2,1,0:T(8,128)(2,1)} %param.10) | copy-start | bytes 786436
  10.5 0.7 copy-start.4
  11.2 0.7 copy-start.5
  11.9 0.7 copy-start.6
  12.5 31.7 %copy-start.1 = (bf16[1,512,1536]{2,1,0:T(8,128)(2,1)S(1)}, bf16[1,512,1536]{2,1,0:T(8,128)(2,1)}, u32[]{:S(2)}) copy-start(bf16[1,512,1536]{2,1,0:T(8,128)(2,1)} %param.12) | copy-start | bytes 4718596
  12.6 31.7 %copy-start.8 = (bf16[1,512,512]{2,1,0:T(8,128)(2,1)S(1)}, bf16[1,512,512]{2,1,0:T(8,128)(2,1)}, u32[]{:S(2)}) copy-start(bf16[1,512,512]{2,1,0:T(8,128)(2,1)} %param.13) | copy-start | bytes 1572868
  14.7 0.8 %copy-start.9 = (f32[2,512,128]{2,1,0:T(8,128)}, f32[2,512,128]{2,1,0:T(8,128)S(1)}, u32[]{:S(2)}) copy-start(f32[2,512,128]{2,1,0:T(8,128)S(1)} %get-tuple-element.12.num_ref) | copy-start | bytes 1572868
  15.5 0.8 %copy-start.11 = (bf16[512,512]{1,0:T(8,128)(2,1)}, bf16[512,512]{1,0:T(8,128)(2,1)S(1)}, u32[]{:S(2)}) copy-start(bf16[512,512]{1,0:T(8,128)(2,1)S(1)} %get-tuple-element.10.wvt_ref) | copy-start | bytes 1572868
  44.2 1.0 %copy-start.10 = (f32[2,512,128]{2,1,0:T(8,128)S(1)}, f32[2,512,128]{2,1,0:T(8,128)}, u32[]{:S(2)}) copy-start(f32[2,512,128]{2,1,0:T(8,128)} %copy-done.9) | copy-start | bytes 1572868
  45.3 1.0 %copy-start.12 = (bf16[512,512]{1,0:T(8,128)(2,1)S(1)}, bf16[512,512]{1,0:T(8,128)(2,1)}, u32[]{:S(2)}) copy-start(bf16[512,512]{1,0:T(8,128)(2,1)} %copy-done.11) | copy-start | bytes 1572868
  56.7 8.3 %collective-permute-start = (bf16[1,256,512]{2,1,0:T(8,128)(2,1)S(1)}, bf16[1,256,512]{2,1,0:T(8,128)(2,1)S(1)}, u32[]{:S(2)}, u32[]{:S(2)}) collective-permute-start(bf16[1,256,512]{2,1,0:T(8,128)(2,1)S(1)} %bitcast.11), channel_id=1, source_target_pairs={{0,8},{8,16},{16,24},{24,0},{1,9},{9,17},{17,25},{25,1},{2,10},{10... | collective-permute-start | bytes 786440 | tf_op jit(solution)/shard_map/ppermute | solution.py:24
Sparse Core Ops, SparseCore 0:
  9.0 35.1 all-gather.1
